TPU v7x, 32 devices: a whole 2x2x4 slice. The times are simulated.
32 devices in a mesh: dp: 8 (over z, x), tensor: 4 (over y, core).
Axes of the slice: x: 2, y: 2, z: 4, core: 2. Of those that a mesh axis runs over, the one named last changes fastest.
Arguments:
- images: bfloat16 [24, 729, 1152], P('dp', None, 'tensor'), may hold values from -6 to 6
- image_count: int32 [8], P('dp'), may hold values from 2 to 3, as said below
- attn_gain: float32 [1152], replicated, may hold values from 0.5 to 1.5
- attn_shift: float32 [1152], replicated, may hold values from -1.8 to 1.8
- query_weight: bfloat16 [1152, 1152], P('dp', 'tensor'), may hold values from -0.25 to 0.25
- query_bias: float32 [1152], P('tensor'), may hold values from -3 to 3
- key_weight: bfloat16 [1152, 1152], P('dp', 'tensor'), may hold values from -0.25 to 0.25
- value_weight: bfloat16 [1152, 1152], P('dp', 'tensor'), may hold values from -0.1875 to 0.1875
- value_bias: float32 [1152], P('tensor'), may hold values from -3 to 3
- output_weight: bfloat16 [1152, 1152], P('tensor', 'dp'), may hold values from -1 to 1
- output_bias: float32 [1152], P('tensor'), may hold values from -3 to 3
- mlp_gain: float32 [1152], replicated, may hold values from 0.5 to 1.5
- mlp_shift: float32 [1152], replicated, may hold values from -1.8 to 1.8
- up_weight: bfloat16 [1152, 4304], P('dp', 'tensor'), may hold values from -0.1875 to 0.1875
- up_bias: float32 [4304], P('tensor'), may hold values from -3 to 3
- down_weight: bfloat16 [4304, 1152], P('tensor', 'dp'), may hold values from -0.125 to 0.125
- down_bias: float32 [1152], P('tensor'), may hold values from -3 to 3
- cotangent: bfloat16 [24, 729, 1152], P('dp', None, 'tensor'), may hold values from -6 to 6
Outputs:
- layer_out: bfloat16 [24, 729, 1152], P('dp', None, 'tensor')
- image_grad: bfloat16 [24, 729, 1152], P('dp', None, 'tensor')
- attn_gain_grad: float32 [1152], P('tensor')
- attn_shift_grad: float32 [1152], P('tensor')
- query_weight_grad: float32 [1152, 1152], P('dp', 'tensor')
- query_bias_grad: float32 [1152], P('tensor')
- key_weight_grad: float32 [1152, 1152], P('dp', 'tensor')
- value_weight_grad: float32 [1152, 1152], P('dp', 'tensor')
- value_bias_grad: float32 [1152], P('tensor')
- output_weight_grad: float32 [1152, 1152], P('tensor', 'dp')
- output_bias_grad: float32 [1152], P('tensor')
- mlp_gain_grad: float32 [1152], P('tensor')
- mlp_shift_grad: float32 [1152], P('tensor')
- up_weight_grad: float32 [1152, 4304], P('dp', 'tensor')
- up_bias_grad: float32 [4304], P('tensor')
- down_weight_grad: float32 [4304, 1152], P('tensor', 'dp')
- down_bias_grad: float32 [1152], P('tensor')
Inputs may be any that keep to these rules, and one draw needn't show every extreme that they name: Slots 0 to image_count - 1 of a data position hold its images; some position has 3 images and some has 2.
All inputs are finite; a program needn't handle non-finite values.
Results may differ from a plain program's by a relative error of at most 0.017.
Values may be sent and summed in bfloat16 or wider, within the bound.
No kernel may reach another device: no remote copies, remote signals or barrier semaphores. Data moves between devices by JAX's collectives and lax.ppermute only.
A program may use at most 256 MiB of HBM per device.

v0:
```python
import math
import jax
import jax.numpy as jnp
from jax import lax
from jax.sharding import PartitionSpec as P

HDIM = 72
EPSILON = 1e-06


def gelu_tanh(value):
    return jax.nn.gelu(value, approximate=True)


def fetch_weights(query_weight, key_weight, value_weight, up_weight, output_weight, down_weight):
    row_parts = (
        lax.all_gather(query_weight, "dp", axis=0, tiled=True),
        lax.all_gather(key_weight, "dp", axis=0, tiled=True),
        lax.all_gather(value_weight, "dp", axis=0, tiled=True),
        lax.all_gather(up_weight, "dp", axis=0, tiled=True),
    )
    col_parts = (
        lax.all_gather(output_weight, "dp", axis=1, tiled=True),
        lax.all_gather(down_weight, "dp", axis=1, tiled=True),
    )
    return tuple(row_parts) + tuple(col_parts)


def normalize(rows):
    centred = rows - jnp.mean(rows, axis=1, keepdims=True)
    inverse = lax.rsqrt(jnp.mean(centred * centred, axis=1, keepdims=True) + EPSILON)
    return (centred * inverse, inverse)


def norm_back(grad_share, normed_share, inverse, gain_share):
    scaled = grad_share * gain_share
    totals = lax.psum((jnp.sum(scaled, axis=1), jnp.sum(scaled * normed_share, axis=1)), "tensor")
    width = grad_share.shape[1] * lax.axis_size("tensor")
    first_mean = totals[0][:, None] / width
    second_mean = totals[1][:, None] / width
    return inverse * (scaled - first_mean - normed_share * second_mean)


def split_heads(rows):
    return rows.reshape(rows.shape[0], -1, HDIM).transpose(1, 0, 2)


def merge_heads(blocks):
    return blocks.transpose(1, 0, 2).reshape(blocks.shape[1], -1)


def column_share(whole, start, width):
    return lax.dynamic_slice_in_dim(whole, start, width, whole.ndim - 1)


def local(
    images,
    image_count,
    attn_gain,
    attn_shift,
    query_weight,
    query_bias,
    key_weight,
    value_weight,
    value_bias,
    output_weight,
    output_bias,
    mlp_gain,
    mlp_shift,
    up_weight,
    up_bias,
    down_weight,
    down_bias,
    cotangent,
):
    share_width = images.shape[2]
    share_start = lax.axis_index("tensor") * share_width
    attn_gain_share = column_share(attn_gain, share_start, share_width)
    mlp_gain_share = column_share(mlp_gain, share_start, share_width)
    score_scale = 1.0 / math.sqrt(HDIM)
    grads_sum = None
    out_slots = []
    grad_slots = []
    for slot_index in range(images.shape[0]):
        weights_now = fetch_weights(
            query_weight, key_weight, value_weight, up_weight, output_weight, down_weight
        )
        query_full, key_full, value_full, up_full, output_full, down_full = weights_now
        live_flag = (image_count[0] > slot_index).astype(jnp.float32)
        rows_pair = (
            lax.all_gather(images[slot_index], "tensor", axis=1, tiled=True),
            lax.all_gather(cotangent[slot_index], "tensor", axis=1, tiled=True),
        )
        input_full = rows_pair[0].astype(jnp.float32)
        grad_full = rows_pair[1].astype(jnp.float32) * live_flag
        grad_low = grad_full.astype(jnp.bfloat16)
        input_share = images[slot_index].astype(jnp.float32)
        grad_share = cotangent[slot_index].astype(jnp.float32) * live_flag
        normed1, inverse1 = normalize(input_full)
        attn_in = (normed1 * attn_gain + attn_shift).astype(jnp.bfloat16)
        query_low = (
            jnp.dot(attn_in, query_full, preferred_element_type=jnp.float32) + query_bias
        ).astype(jnp.bfloat16)
        key_low = jnp.dot(attn_in, key_full, preferred_element_type=jnp.float32).astype(
            jnp.bfloat16
        )
        value_low = (
            jnp.dot(attn_in, value_full, preferred_element_type=jnp.float32) + value_bias
        ).astype(jnp.bfloat16)
        query_heads = split_heads(query_low)
        key_heads = split_heads(key_low)
        value_heads = split_heads(value_low)
        scores = (
            jnp.einsum("hqd,hkd->hqk", query_heads, key_heads, preferred_element_type=jnp.float32)
            * score_scale
        )
        row_max = jnp.max(scores, axis=-1, keepdims=True)
        expo = jnp.exp(scores - row_max)
        prob_total = jnp.sum(expo, axis=-1, keepdims=True)
        log_total = row_max + jnp.log(prob_total)
        probs_low = (expo / prob_total).astype(jnp.bfloat16)
        mixed_heads = jnp.einsum(
            "hqk,hkd->hqd", probs_low, value_heads, preferred_element_type=jnp.float32
        )
        mixed_low = merge_heads(mixed_heads).astype(jnp.bfloat16)
        attn_partial = jnp.dot(mixed_low, output_full, preferred_element_type=jnp.float32)
        attn_share = lax.psum_scatter(attn_partial, "tensor", scatter_dimension=1, tiled=True)
        hidden1_share = input_share + attn_share + output_bias
        hidden1_full = lax.all_gather(hidden1_share, "tensor", axis=1, tiled=True)
        normed2, inverse2 = normalize(hidden1_full)
        mlp_in = (normed2 * mlp_gain + mlp_shift).astype(jnp.bfloat16)
        pre_act = jnp.dot(mlp_in, up_full, preferred_element_type=jnp.float32) + up_bias
        activ, gelu_pull = jax.vjp(gelu_tanh, pre_act)
        activ_low = activ.astype(jnp.bfloat16)
        mlp_partial = jnp.dot(activ_low, down_full, preferred_element_type=jnp.float32)
        mlp_share = lax.psum_scatter(
            mlp_partial.astype(jnp.bfloat16), "tensor", scatter_dimension=1, tiled=True
        ).astype(jnp.float32)
        out_slots.append(((hidden1_share + mlp_share + down_bias) * live_flag).astype(jnp.bfloat16))
        down_grad = jnp.einsum("sf,sd->fd", activ_low, grad_low, preferred_element_type=jnp.float32)
        hidden_grad = jnp.einsum(
            "sd,fd->sf", grad_low, down_full, preferred_element_type=jnp.float32
        )
        pre_grad = gelu_pull(hidden_grad)[0].astype(jnp.bfloat16)
        up_grad = jnp.einsum("sd,sf->df", mlp_in, pre_grad, preferred_element_type=jnp.float32)
        norm2_partial = jnp.einsum(
            "sf,df->sd", pre_grad, up_full, preferred_element_type=jnp.float32
        )
        normed2_share = column_share(normed2, share_start, share_width)
        norm2_share = lax.psum_scatter(norm2_partial, "tensor", scatter_dimension=1, tiled=True)
        hidden1_grad = grad_share + norm_back(norm2_share, normed2_share, inverse2, mlp_gain_share)
        branch_low = lax.all_gather(hidden1_grad.astype(jnp.bfloat16), "tensor", axis=1, tiled=True)
        output_grad = jnp.einsum(
            "sh,sd->hd", mixed_low, branch_low, preferred_element_type=jnp.float32
        )
        mixed_grad = split_heads(
            jnp.einsum(
                "sd,hd->sh", branch_low, output_full, preferred_element_type=jnp.float32
            ).astype(jnp.bfloat16)
        )
        scores_again = (
            jnp.einsum("hqd,hkd->hqk", query_heads, key_heads, preferred_element_type=jnp.float32)
            * score_scale
        )
        probs_again = jnp.exp(scores_again - log_total)
        probs_again_low = probs_again.astype(jnp.bfloat16)
        prob_grad = jnp.einsum(
            "hqd,hkd->hqk", mixed_grad, value_heads, preferred_element_type=jnp.float32
        )
        row_delta = jnp.sum(probs_again * prob_grad, axis=-1, keepdims=True)
        score_grad = (probs_again * (prob_grad - row_delta)).astype(jnp.bfloat16)
        query_grad = merge_heads(
            jnp.einsum("hqk,hkd->hqd", score_grad, key_heads, preferred_element_type=jnp.float32)
            * score_scale
        ).astype(jnp.bfloat16)
        key_grad = merge_heads(
            jnp.einsum("hqk,hqd->hkd", score_grad, query_heads, preferred_element_type=jnp.float32)
            * score_scale
        ).astype(jnp.bfloat16)
        value_grad = merge_heads(
            jnp.einsum(
                "hqk,hqd->hkd", probs_again_low, mixed_grad, preferred_element_type=jnp.float32
            )
        ).astype(jnp.bfloat16)
        query_w_grad = jnp.einsum(
            "sd,sh->dh", attn_in, query_grad, preferred_element_type=jnp.float32
        )
        key_w_grad = jnp.einsum("sd,sh->dh", attn_in, key_grad, preferred_element_type=jnp.float32)
        value_w_grad = jnp.einsum(
            "sd,sh->dh", attn_in, value_grad, preferred_element_type=jnp.float32
        )
        norm1_partial = jnp.einsum(
            "sh,dh->sd", query_grad, query_full, preferred_element_type=jnp.float32
        )
        norm1_partial = norm1_partial + jnp.einsum(
            "sh,dh->sd", key_grad, key_full, preferred_element_type=jnp.float32
        )
        norm1_partial = norm1_partial + jnp.einsum(
            "sh,dh->sd", value_grad, value_full, preferred_element_type=jnp.float32
        )
        norm1_share = lax.psum_scatter(
            norm1_partial.astype(jnp.bfloat16), "tensor", scatter_dimension=1, tiled=True
        ).astype(jnp.float32)
        normed1_share = column_share(normed1, share_start, share_width)
        grad_slots.append(
            (
                hidden1_grad + norm_back(norm1_share, normed1_share, inverse1, attn_gain_share)
            ).astype(jnp.bfloat16)
        )
        slot_grads = (
            query_w_grad,
            key_w_grad,
            value_w_grad,
            up_grad,
            output_grad,
            down_grad,
            jnp.sum(norm1_share * normed1_share, axis=0),
            jnp.sum(norm1_share, axis=0),
            jnp.sum(query_grad.astype(jnp.float32), axis=0),
            jnp.sum(value_grad.astype(jnp.float32), axis=0),
            jnp.sum(hidden1_grad, axis=0),
            jnp.sum(norm2_share * normed2_share, axis=0),
            jnp.sum(norm2_share, axis=0),
            jnp.sum(pre_grad.astype(jnp.float32), axis=0),
            jnp.sum(grad_share, axis=0),
        )
        grads_sum = (
            slot_grads if grads_sum is None else jax.tree.map(jnp.add, grads_sum, slot_grads)
        )
    row_grads = (
        lax.psum_scatter(grads_sum[0], "dp", scatter_dimension=0, tiled=True),
        lax.psum_scatter(grads_sum[1], "dp", scatter_dimension=0, tiled=True),
        lax.psum_scatter(grads_sum[2], "dp", scatter_dimension=0, tiled=True),
        lax.psum_scatter(grads_sum[3], "dp", scatter_dimension=0, tiled=True),
    )
    col_grads = (
        lax.psum_scatter(grads_sum[4], "dp", scatter_dimension=1, tiled=True),
        lax.psum_scatter(grads_sum[5], "dp", scatter_dimension=1, tiled=True),
    )
    small = lax.psum(
        (
            grads_sum[6],
            grads_sum[7],
            grads_sum[8],
            grads_sum[9],
            grads_sum[10],
            grads_sum[11],
            grads_sum[12],
            grads_sum[13],
            grads_sum[14],
        ),
        "dp",
    )
    return (
        jnp.stack(out_slots),
        jnp.stack(grad_slots),
        small[0],
        small[1],
        row_grads[0],
        small[2],
        row_grads[1],
        row_grads[2],
        small[3],
        col_grads[0],
        small[4],
        small[5],
        small[6],
        row_grads[3],
        small[7],
        col_grads[1],
        small[8],
    )


def solution(mesh):
    in_specs = (
        P("dp", None, "tensor"),
        P("dp"),
        P(),
        P(),
        P("dp", "tensor"),
        P("tensor"),
        P("dp", "tensor"),
        P("dp", "tensor"),
        P("tensor"),
        P("tensor", "dp"),
        P("tensor"),
        P(),
        P(),
        P("dp", "tensor"),
        P("tensor"),
        P("tensor", "dp"),
        P("tensor"),
        P("dp", None, "tensor"),
    )
    out_specs = (
        P("dp", None, "tensor"),
        P("dp", None, "tensor"),
        P("tensor"),
        P("tensor"),
        P("dp", "tensor"),
        P("tensor"),
        P("dp", "tensor"),
        P("dp", "tensor"),
        P("tensor"),
        P("tensor", "dp"),
        P("tensor"),
        P("tensor"),
        P("tensor"),
        P("dp", "tensor"),
        P("tensor"),
        P("tensor", "dp"),
        P("tensor"),
    )
    return jax.shard_map(local, mesh=mesh, in_specs=in_specs, out_specs=out_specs, check_vma=False)
```

profile of v0, /device:TPU:0, one launch (start us, length us, event | category | flops | bytes accessed | tf_op | source)
XLA Modules:
  0.0 1480.5 jit_solution(229131202090913659)
XLA Ops:
  11.3 34.3 %all_gather.67 = bf16[1152,288]{1,0:T(8,128)(2,1)S(1)} all-gather(bf16[144,288]{1,0:T(8,128)(2,1)S(1)} %copy-done.91), channel_id=1, replica_groups=mesh['dp'=8,'tensor'=4] {'dp'}, dimensions={0}, use_global_device_ids=true | all-gather | bytes 746496 | tf_op jit(solution)/shard_map/all_gather | solution.py:17
  45.6 32.7 %all_gather.68 = bf16[1152,288]{1,0:T(8,128)(2,1)S(1)} all-gather(bf16[144,288]{1,0:T(8,128)(2,1)S(1)} %copy-done.92), channel_id=1, replica_groups=mesh['dp'=8,'tensor'=4] {'dp'}, dimensions={0}, use_global_device_ids=true | all-gather | bytes 746496 | tf_op jit(solution)/shard_map/all_gather | solution.py:18
  78.3 32.3 %all_gather.69 = bf16[1152,288]{1,0:T(8,128)(2,1)S(1)} all-gather(bf16[144,288]{1,0:T(8,128)(2,1)S(1)} %copy-done.93), channel_id=1, replica_groups=mesh['dp'=8,'tensor'=4] {'dp'}, dimensions={0}, use_global_device_ids=true | all-gather | bytes 746496 | tf_op jit(solution)/shard_map/all_gather | solution.py:19
  110.6 32.1 %all_gather.70 = bf16[288,1152]{0,1:T(8,128)(2,1)S(1)} all-gather(bf16[288,144]{0,1:T(8,128)(2,1)} %param.27), channel_id=1, replica_groups=mesh['dp'=8,'tensor'=4] {'dp'}, dimensions={1}, use_global_device_ids=true | all-gather | bytes 746496 | tf_op jit(solution)/shard_map/all_gather | solution.py:23
  204.2 43.1 %reduce-scatter.27.cloned.1.call-done = f32[729,288]{0,1:T(8,128)} async-done(((f32[729,1152]{0,1:T(8,128)}), f32[729,288]{0,1:T(8,128)}) %reduce-scatter.27.cloned.1.call-update) | async-done | bytes 839824 | tf_op jit(solution)/shard_map/reduce_scatter | solution.py:127
  247.3 42.9 %reduce-scatter.19.cloned.1.call-done = f32[729,288]{0,1:T(8,128)} async-done(((f32[729,1152]{0,1:T(8,128)}), f32[729,288]{0,1:T(8,128)}) %reduce-scatter.19.cloned.1.call-update) | async-done | bytes 839824 | tf_op jit(solution)/shard_map/reduce_scatter | solution.py:127
  299.8 24.9 %all-gather.29.cloned.1.call-done = f32[729,1152]{0,1:T(8,128)} async-done(((f32[729,288]{0,1:T(8,128)}), f32[729,1152]{0,1:T(8,128)}) %all-gather.29.cloned.1.call-update) | async-done | bytes 3359248 | tf_op jit(solution)/shard_map/all_gather | solution.py:129
  330.3 51.8 %all-gather.23.cloned.1.call-done = bf16[1152,1076]{1,0:T(8,128)(2,1)} async-done(((bf16[144,1076]{1,0:T(8,128)(2,1)}), bf16[1152,1076]{1,0:T(8,128)(2,1)}) %all-gather.23.cloned.1.call-update) | async-done | bytes 2479120 | tf_op jit(solution)/shard_map/all_gather | solution.py:20
  387.6 16.2 %all-gather.47.cloned.1.call-done = bf16[1,729,1152]{1,2,0:T(8,128)(2,1)} async-done(((bf16[1,729,288]{1,2,0:T(8,128)(2,1)}), bf16[1,729,1152]{1,2,0:T(8,128)(2,1)}) %all-gather.47.cloned.1.call-update) | async-done | bytes 1679632 | tf_op jit(solution)/shard_map/all_gather | solution.py:92
  403.7 57.3 %all-gather.25.cloned.1.call-done = bf16[1076,1152]{0,1:T(8,128)(2,1)} async-done(((bf16[1076,144]{0,1:T(8,128)(2,1)}), bf16[1076,1152]{0,1:T(8,128)(2,1)}) %all-gather.25.cloned.1.call-update) | async-done | bytes 2479120 | tf_op jit(solution)/shard_map/all_gather | solution.py:24
  474.5 18.2 %all-gather.27.cloned.1.call-done = f32[729,1152]{0,1:T(8,128)} async-done(((f32[729,288]{0,1:T(8,128)}), f32[729,1152]{0,1:T(8,128)}) %all-gather.27.cloned.1.call-update) | async-done | bytes 3359248 | tf_op jit(solution)/shard_map/all_gather | solution.py:129
  528.4 19.5 %all-gather.21.cloned.1.call-done = f32[729,1152]{0,1:T(8,128)} async-done(((f32[729,288]{0,1:T(8,128)}), f32[729,1152]{0,1:T(8,128)}) %all-gather.21.cloned.1.call-update) | async-done | bytes 3359248 | tf_op jit(solution)/shard_map/all_gather | solution.py:129
  585.0 28.9 %reduce-scatter.39.cloned.1.call-done = f32[729,288]{0,1:T(8,128)} async-done(((f32[729,1152]{0,1:T(8,128)}), f32[729,288]{0,1:T(8,128)}) %reduce-scatter.39.cloned.1.call-update) | async-done | bytes 839824 | tf_op jit(solution)/shard_map/reduce_scatter | solution.py:150
  613.9 42.9 %reduce-scatter.35.cloned.1.call-done = f32[729,288]{0,1:T(8,128)} async-done(((f32[729,1152]{0,1:T(8,128)}), f32[729,288]{0,1:T(8,128)}) %reduce-scatter.35.cloned.1.call-update) | async-done | bytes 839824 | tf_op jit(solution)/shard_map/reduce_scatter | solution.py:150
  656.7 43.0 %reduce-scatter.31.cloned.1.call-done = f32[729,288]{0,1:T(8,128)} async-done(((f32[729,1152]{0,1:T(8,128)}), f32[729,288]{0,1:T(8,128)}) %reduce-scatter.31.cloned.1.call-update) | async-done | bytes 839824 | tf_op jit(solution)/shard_map/reduce_scatter | solution.py:150
  919.0 27.4 %reduce-scatter.41.cloned.1.call-done = bf16[729,288]{0,1:T(8,128)(2,1)} async-done(((bf16[729,1152]{0,1:T(8,128)(2,1)}), bf16[729,288]{0,1:T(8,128)(2,1)}) %reduce-scatter.41.cloned.1.call-update) | async-done | bytes 419920 | tf_op jit(solution)/shard_map/reduce_scatter | solution.py:201
  946.4 32.0 %reduce-scatter.37.cloned.1.call-done = bf16[729,288]{0,1:T(8,128)(2,1)} async-done(((bf16[729,1152]{0,1:T(8,128)(2,1)}), bf16[729,288]{0,1:T(8,128)(2,1)}) %reduce-scatter.37.cloned.1.call-update) | async-done | bytes 419920 | tf_op jit(solution)/shard_map/reduce_scatter | solution.py:201
  983.4 40.5 %all-reduce = (f32[288]{0:T(512)}, f32[288]{0:T(512)}, f32[288]{0:T(512)}, f32[288]{0:T(512)}, f32[288]{0:T(512)}, /*index=5*/f32[288]{0:T(512)}, f32[288]{0:T(512)}, f32[1076]{0:T(1024)}, f32[288]{0:T(512)}) all-reduce(f32[288]{0:T(512)} %add_add_fusion.8, f32[288]{0:T(512)} %add_add_fusion.7, ...), channel_id=1, replica_groups=mesh['dp'=8,'tensor'=4] {'dp'}, use_global_device_ids=true, to_apply=%region_60.0 | all-reduce | flops 3380 | bytes 27040 | tf_op jit(solution)/shard_map/psum | solution.py:240
  1045.0 42.1 %reduce-scatter.53.cloned.1.call-done = f32[1076,144]{0,1:T(8,128)} async-done(((f32[1076,1152]{0,1:T(8,128)}), f32[1076,144]{0,1:T(8,128)}) %reduce-scatter.53.cloned.1.call-update) | async-done | bytes 619792 | tf_op jit(solution)/shard_map/reduce_scatter | solution.py:238
  1087.2 108.6 %reduce-scatter.51.cloned.1.call-done = f32[144,1076]{1,0:T(8,128)} async-done(((f32[1152,1076]{1,0:T(8,128)}), f32[144,1076]{1,0:T(8,128)}) %reduce-scatter.51.cloned.1.call-update) | async-done | bytes 619792 | tf_op jit(solution)/shard_map/reduce_scatter | solution.py:234
  1195.7 69.7 %reduce-scatter.49.cloned.1.call-done = f32[288,144]{0,1:T(8,128)} async-done(((f32[288,1152]{0,1:T(8,128)}), f32[288,144]{0,1:T(8,128)}) %reduce-scatter.49.cloned.1.call-update) | async-done | bytes 165904 | tf_op jit(solution)/shard_map/reduce_scatter | solution.py:237
  1265.5 69.7 %reduce-scatter.47.cloned.1.call-done = f32[144,288]{1,0:T(8,128)} async-done(((f32[1152,288]{1,0:T(8,128)}), f32[144,288]{1,0:T(8,128)}) %reduce-scatter.47.cloned.1.call-update) | async-done | bytes 165904 | tf_op jit(solution)/shard_map/reduce_scatter | solution.py:233
  1335.2 69.2 %reduce-scatter.43.cloned.1.call-done = f32[144,288]{1,0:T(8,128)} async-done(((f32[1152,288]{1,0:T(8,128)}), f32[144,288]{1,0:T(8,128)}) %reduce-scatter.43.cloned.1.call-update) | async-done | bytes 165904 | tf_op jit(solution)/shard_map/reduce_scatter | solution.py:231
  1404.3 69.4 %reduce-scatter.45.cloned.1.call-done = f32[144,288]{1,0:T(8,128)} async-done(((f32[1152,288]{1,0:T(8,128)}), f32[144,288]{1,0:T(8,128)}) %reduce-scatter.45.cloned.1.call-update) | async-done | bytes 165904 | tf_op jit(solution)/shard_map/reduce_scatter | solution.py:232
  (550 shorter events, 414.8 us)
Async XLA Ops:
  9.7 152.9 %all-gather.41.cloned.1.call-start = ((), (), s32[]{:S(2)}) async-start(), calls=%async_computation.46 | async-start | bytes 2211840 | tf_op jit(solution)/shard_map/all_gather | solution.py:91
  10.5 172.1 %all-gather.37.cloned.1.call-start = ((), (), s32[]{:S(2)}) async-start(), calls=%async_computation.44 | async-start | bytes 2211840 | tf_op jit(solution)/shard_map/all_gather | solution.py:91
  11.2 193.0 %reduce-scatter.23.cloned.1.call-start = ((), (), s32[]{:S(2)}) async-start(), calls=%async_computation.23 | async-start | bytes 4423680 | tf_op jit(solution)/shard_map/reduce_scatter | solution.py:127
  295.7 165.4 %all-gather.25.cloned.1.call-start = ((), (), s32[]{:S(2)}) async-start(), calls=%async_computation.21 | async-start | bytes 2985984 | tf_op jit(solution)/shard_map/all_gather | solution.py:24
  296.3 196.4 %all-gather.27.cloned.1.call-start = ((), (), s32[]{:S(2)}) async-start(), calls=%async_computation.24 | async-start | bytes 4423680 | tf_op jit(solution)/shard_map/all_gather | solution.py:129
  297.0 217.9 %all-gather.45.cloned.1.call-start = ((), (), s32[]{:S(2)}) async-start(), calls=%async_computation.48 | async-start | bytes 2211840 | tf_op jit(solution)/shard_map/all_gather | solution.py:92
  297.6 250.4 %all-gather.21.cloned.1.call-start = ((), (), s32[]{:S(2)}) async-start(), calls=%async_computation.19 | async-start | bytes 4423680 | tf_op jit(solution)/shard_map/all_gather | solution.py:129
  298.3 272.5 %all-gather.43.cloned.1.call-start = ((), (), s32[]{:S(2)}) async-start(), calls=%async_computation.47 | async-start | bytes 2211840 | tf_op jit(solution)/shard_map/all_gather | solution.py:92
  298.9 314.9 %reduce-scatter.39.cloned.1.call-start = ((), (), s32[]{:S(2)}) async-start(), calls=%async_computation.35 | async-start | bytes 4423680 | tf_op jit(solution)/shard_map/reduce_scatter | solution.py:150
  474.0 182.7 %reduce-scatter.35.cloned.1.call-start = ((), (), s32[]{:S(2)}) async-start(), calls=%async_computation.32 | async-start | bytes 4423680 | tf_op jit(solution)/shard_map/reduce_scatter | solution.py:150
  528.2 171.6 %reduce-scatter.31.cloned.1.call-start = ((), (), s32[]{:S(2)}) async-start(), calls=%async_computation.29 | async-start | bytes 4423680 | tf_op jit(solution)/shard_map/reduce_scatter | solution.py:150
  584.0 161.5 %all-gather.31.cloned.1.call-start = ((), (), s32[]{:S(2)}) async-start(), calls=%async_computation.30 | async-start | bytes 2211840 | tf_op jit(solution)/shard_map/all_gather | solution.py:152
  724.0 179.7 %reduce-scatter.21.cloned.1.call-start = ((), (), s32[]{:S(2)}) async-start(), calls=%async_computation.22 | async-start | bytes 2211840 | tf_op jit(solution)/shard_map/reduce_scatter | solution.py:136
  730.8 172.8 %reduce-scatter.25.cloned.1.call-start = ((), (), s32[]{:S(2)}) async-start(), calls=%async_computation.25 | async-start | bytes 2211840 | tf_op jit(solution)/shard_map/reduce_scatter | solution.py:136
  737.5 166.2 %reduce-scatter.29.cloned.1.call-start = ((), (), s32[]{:S(2)}) async-start(), calls=%async_computation.28 | async-start | bytes 2211840 | tf_op jit(solution)/shard_map/reduce_scatter | solution.py:136
  745.1 173.9 %reduce-scatter.33.cloned.1.call-start = ((), (), s32[]{:S(2)}) async-start(), calls=%async_computation.31 | async-start | bytes 2211840 | tf_op jit(solution)/shard_map/reduce_scatter | solution.py:201
  780.1 166.3 %reduce-scatter.41.cloned.1.call-start = ((), (), s32[]{:S(2)}) async-start(), calls=%async_computation.37 | async-start | bytes 2211840 | tf_op jit(solution)/shard_map/reduce_scatter | solution.py:201
  815.4 163.0 %reduce-scatter.37.cloned.1.call-start = ((), (), s32[]{:S(2)}) async-start(), calls=%async_computation.34 | async-start | bytes 2211840 | tf_op jit(solution)/shard_map/reduce_scatter | solution.py:201
  850.3 236.9 %reduce-scatter.53.cloned.1.call-start = ((), (), s32[]{:S(2)}) async-start(), calls=%async_computation.43 | async-start | bytes 5971968 | tf_op jit(solution)/shard_map/reduce_scatter | solution.py:238
  863.6 332.2 %reduce-scatter.51.cloned.1.call-start = ((), (), s32[]{:S(2)}) async-start(), calls=%async_computation.42 | async-start | bytes 5971968 | tf_op jit(solution)/shard_map/reduce_scatter | solution.py:234
  877.9 387.6 %reduce-scatter.49.cloned.1.call-start = ((), (), s32[]{:S(2)}) async-start(), calls=%async_computation.41 | async-start | bytes 1990656 | tf_op jit(solution)/shard_map/reduce_scatter | solution.py:237
  885.5 449.7 %reduce-scatter.47.cloned.1.call-start = ((), (), s32[]{:S(2)}) async-start(), calls=%async_computation.40 | async-start | bytes 1990656 | tf_op jit(solution)/shard_map/reduce_scatter | solution.py:233
  892.8 511.6 %reduce-scatter.43.cloned.1.call-start = ((), (), s32[]{:S(2)}) async-start(), calls=%async_computation.38 | async-start | bytes 1990656 | tf_op jit(solution)/shard_map/reduce_scatter | solution.py:231
  902.3 571.5 %reduce-scatter.45.cloned.1.call-start = ((), (), s32[]{:S(2)}) async-start(), calls=%async_computation.39 | async-start | bytes 1990656 | tf_op jit(solution)/shard_map/reduce_scatter | solution.py:232
  (168 other events, 3241.5 us)
Sparse Core Ops, SparseCore 0:
  10.2 23.4 all-gather.38
  162.2 41.9 reduce-scatter.22
  206.8 40.4 reduce-scatter.26
  249.7 40.4 reduce-scatter.18
  293.9 30.7 all-gather.28
  327.1 55.0 all-gather.22
  406.0 55.0 all-gather.24
  463.3 29.3 all-gather.26
  517.1 30.7 all-gather.20
  573.4 40.4 reduce-scatter.38
  616.3 40.4 reduce-scatter.34
  659.3 40.4 reduce-scatter.30
  788.8 29.4 reduce-scatter.20
  821.1 29.3 reduce-scatter.24
  853.0 29.3 reduce-scatter.28
  885.0 29.3 reduce-scatter.32
  917.0 29.3 reduce-scatter.40
  949.0 29.3 reduce-scatter.36
  982.5 104.6 reduce-scatter.52
  1091.8 103.9 reduce-scatter.50
  1199.8 65.6 reduce-scatter.48
  1269.8 65.3 reduce-scatter.46
  1339.2 65.0 reduce-scatter.42
  1408.8 64.9 reduce-scatter.44
  (8 shorter events, 165.3 us)
where the time goes:
time: 1490 us; the launch traced here: 1480 us
  waiting for transfers between devices  908 us (61%)
  matrix products  214 us (14%)
  blocking collectives  195 us (13%)
  other arithmetic  108 us (7%)
  local copies, waits for them, and re-layouts  34.3 us (2%)
  between operations  17 us (1%)
    reduce_scatter x3, waiting for transfers between devices, local(): lax.psum_scatter(norm2_partial, 'tensor', scatter_dimension=1, tiled=True)  115 us
    reduce_scatter x1, waiting for transfers between devices, local(): lax.psum_scatter(grads_sum[3], 'dp', scatter_dimension=0, tiled=True)  109 us
    reduce_scatter x3, waiting for transfers between devices, local(): lax.psum_scatter(attn_partial, 'tensor', scatter_dimension=1, tiled=True)  87.7 us
    reduce_scatter x1, waiting for transfers between devices, local(): lax.psum_scatter(grads_sum[4], 'dp', scatter_dimension=1, tiled=True)  69.7 us
    reduce_scatter x1, waiting for transfers between devices, local(): lax.psum_scatter(grads_sum[2], 'dp', scatter_dimension=0, tiled=True)  69.7 us
    reduce_scatter x1, waiting for transfers between devices, local(): lax.psum_scatter(grads_sum[1], 'dp', scatter_dimension=0, tiled=True)  69.4 us
    reduce_scatter x1, waiting for transfers between devices, local(): lax.psum_scatter(grads_sum[0], 'dp', scatter_dimension=0, tiled=True)  69.2 us
    all_gather x3, waiting for transfers between devices, local(): hidden1_full = lax.all_gather(hidden1_share, 'tensor', axis=1, tiled=True)  62.6 us
  transfers between devices with their start and end apart: 32, of which 22 were waited for; matrix products, arithmetic and copies ran while one was open for 21% of the time, Pallas kernels for 0%

commit v1 on v0

--- a/solution.py
+++ b/solution.py
@@ -126,7 +126,16 @@
         attn_partial = jnp.dot(mixed_low, output_full, preferred_element_type=jnp.float32)
         attn_share = lax.psum_scatter(attn_partial, "tensor", scatter_dimension=1, tiled=True)
         hidden1_share = input_share + attn_share + output_bias
-        hidden1_full = lax.all_gather(hidden1_share, "tensor", axis=1, tiled=True)
+        ring = [hidden1_share]
+        for hop in range(3):
+            ring.append(
+                lax.ppermute(ring[-1], "tensor", [(dev, (dev + 1) % 4) for dev in range(4)])
+            )
+        hidden1_full = jnp.roll(
+            jnp.concatenate(ring[::-1], axis=1),
+            (lax.axis_index("tensor") + 1) * ring[0].shape[1],
+            axis=1,
+        )
         normed2, inverse2 = normalize(hidden1_full)
         mlp_in = (normed2 * mlp_gain + mlp_shift).astype(jnp.bfloat16)
         pre_act = jnp.dot(mlp_in, up_full, preferred_element_type=jnp.float32) + up_bias

time: 1490 us -> 1340 us (0.90)
  waiting for transfers between devices: 908 us -> 714 us
  other arithmetic: 108 us -> 131 us
    ppermute x0 -> x9, waiting for transfers between devices: none -> 107 us  [local(): lax.ppermute(ring[-1], 'tensor', [(dev, (dev + 1) % 4) for dev in range(4)])]
    reduce_scatter x3, waiting for transfers between devices: 115 us -> 39.2 us  [local(): lax.psum_scatter(norm2_partial, 'tensor', scatter_dimension=1, tiled=True)]
    all_gather x3 -> x0, waiting for transfers between devices: 62.6 us -> none  [local(): hidden1_full = lax.all_gather(hidden1_share, 'tensor', axis=1, tiled=True)]
    all_gather x1, waiting for transfers between devices: 57.3 us -> 5.36 us  [fetch_weights(): lax.all_gather(down_weight, 'dp', axis=1, tiled=True)]
    all_gather x1, waiting for transfers between devices: 51.8 us -> 0.01 us  [fetch_weights(): lax.all_gather(up_weight, 'dp', axis=0, tiled=True)]
    all_gather x3, waiting for transfers between devices: 39.7 us -> 0.01 us  [local(): lax.all_gather(cotangent[slot_index], 'tensor', axis=1, tiled=True)]
    reduce_sum x6, other arithmetic: 13.3 us -> 29 us  [normalize(): centred = rows - jnp.mean(rows, axis=1, keepdims=True)]
  transfers between devices with their start and end apart: 32 -> 38, of which waited for: 22 -> 19; matrix products, arithmetic and copies ran while one was open for 21% -> 27% of each run, Pallas kernels for 0% -> 0%
where the time goes in v1:
time: 1340 us; the launch traced here: 1330 us
  waiting for transfers between devices  714 us (53%)
  matrix products  228 us (17%)
  blocking collectives  196 us (15%)
  other arithmetic  131 us (10%)
  local copies, waits for them, and re-layouts  34.3 us (3%)
  between operations  18.7 us (1%)
    reduce_scatter x1, waiting for transfers between devices, local(): lax.psum_scatter(grads_sum[3], 'dp', scatter_dimension=0, tiled=True)  108 us
    ppermute x9, waiting for transfers between devices, local(): lax.ppermute(ring[-1], 'tensor', [(dev, (dev + 1) % 4) for dev in range(4)])  107 us
    reduce_scatter x3, waiting for transfers between devices, local(): lax.psum_scatter(attn_partial, 'tensor', scatter_dimension=1, tiled=True)  83.3 us
    reduce_scatter x1, waiting for transfers between devices, local(): lax.psum_scatter(grads_sum[4], 'dp', scatter_dimension=1, tiled=True)  70 us
    reduce_scatter x1, waiting for transfers between devices, local(): lax.psum_scatter(grads_sum[0], 'dp', scatter_dimension=0, tiled=True)  70 us
    reduce_scatter x1, waiting for transfers between devices, local(): lax.psum_scatter(grads_sum[2], 'dp', scatter_dimension=0, tiled=True)  69.7 us
    reduce_scatter x1, waiting for transfers between devices, local(): lax.psum_scatter(grads_sum[1], 'dp', scatter_dimension=0, tiled=True)  69.1 us
    reduce_scatter x3, waiting for transfers between devices, local(): lax.psum_scatter(norm1_partial.astype(jnp.bfloat16), 'tensor', scatter_di...  46.5 us
  transfers between devices with their start and end apart: 38, of which 19 were waited for; matrix products, arithmetic and copies ran while one was open for 27% of the time, Pallas kernels for 0%

profile of v1, /device:TPU:0, one launch (start us, length us, event | category | flops | bytes accessed | tf_op | source)
XLA Modules:
  0.0 1326.2 jit_solution(4408848117064737549)
XLA Ops:
  12.1 34.3 %all_gather.58 = bf16[1152,288]{1,0:T(8,128)(2,1)S(1)} all-gather(bf16[144,288]{1,0:T(8,128)(2,1)S(1)} %copy-done.71), channel_id=1, replica_groups=mesh['dp'=8,'tensor'=4] {'dp'}, dimensions={0}, use_global_device_ids=true | all-gather | bytes 746496 | tf_op jit(solution)/shard_map/all_gather | solution.py:17
  46.4 32.7 %all_gather.59 = bf16[1152,288]{1,0:T(8,128)(2,1)S(1)} all-gather(bf16[144,288]{1,0:T(8,128)(2,1)S(1)} %copy-done.72), channel_id=1, replica_groups=mesh['dp'=8,'tensor'=4] {'dp'}, dimensions={0}, use_global_device_ids=true | all-gather | bytes 746496 | tf_op jit(solution)/shard_map/all_gather | solution.py:18
  79.1 32.3 %all_gather.60 = bf16[1152,288]{1,0:T(8,128)(2,1)S(1)} all-gather(bf16[144,288]{1,0:T(8,128)(2,1)S(1)} %copy-done.73), channel_id=1, replica_groups=mesh['dp'=8,'tensor'=4] {'dp'}, dimensions={0}, use_global_device_ids=true | all-gather | bytes 746496 | tf_op jit(solution)/shard_map/all_gather | solution.py:19
  111.4 32.2 %all_gather.61 = bf16[288,1152]{0,1:T(8,128)(2,1)S(1)} all-gather(bf16[288,144]{0,1:T(8,128)(2,1)} %param.29), channel_id=1, replica_groups=mesh['dp'=8,'tensor'=4] {'dp'}, dimensions={1}, use_global_device_ids=true | all-gather | bytes 746496 | tf_op jit(solution)/shard_map/all_gather | solution.py:23
  207.7 40.1 %reduce-scatter.23.cloned.1.call-done = f32[729,288]{0,1:T(8,128)} async-done(((f32[729,1152]{0,1:T(8,128)}), f32[729,288]{0,1:T(8,128)}) %reduce-scatter.23.cloned.1.call-update) | async-done | bytes 839824 | tf_op jit(solution)/shard_map/reduce_scatter | solution.py:127
  247.9 43.1 %reduce-scatter.19.cloned.1.call-done = f32[729,288]{0,1:T(8,128)} async-done(((f32[729,1152]{0,1:T(8,128)}), f32[729,288]{0,1:T(8,128)}) %reduce-scatter.19.cloned.1.call-update) | async-done | bytes 839824 | tf_op jit(solution)/shard_map/reduce_scatter | solution.py:127
  295.5 12.8 collective-permute-done.6
  309.4 12.6 collective-permute-done.7
  372.2 14.7 %collective-permute-done.4 = f32[729,288]{0,1:T(8,128)S(1)} collective-permute-done((f32[729,288]{0,1:T(8,128)}, f32[729,288]{0,1:T(8,128)S(1)}, u32[]{:S(2)}, u32[]{:S(2)}) %collective-permute-start.4) | collective-permute-done | bytes 839840 | tf_op jit(solution)/shard_map/ppermute | solution.py:132
  387.4 21.5 %collective-permute-done.5 = f32[729,288]{0,1:T(8,128)S(1)} collective-permute-done((f32[729,288]{0,1:T(8,128)S(1)}, f32[729,288]{0,1:T(8,128)S(1)}, u32[]{:S(2)}, u32[]{:S(2)}) %collective-permute-start.5) | collective-permute-done | bytes 839840 | tf_op jit(solution)/shard_map/ppermute | solution.py:132
  438.9 21.4 %collective-permute-done.1 = f32[729,288]{0,1:T(8,128)S(1)} collective-permute-done((f32[729,288]{0,1:T(8,128)}, f32[729,288]{0,1:T(8,128)S(1)}, u32[]{:S(2)}, u32[]{:S(2)}) %collective-permute-start.1) | collective-permute-done | bytes 839840 | tf_op jit(solution)/shard_map/ppermute | solution.py:132
  460.3 12.5 collective-permute-done.2
  503.0 39.2 %reduce-scatter.31.cloned.1.call-done = f32[729,288]{0,1:T(8,128)} async-done(((f32[729,1152]{0,1:T(8,128)}), f32[729,288]{0,1:T(8,128)}) %reduce-scatter.31.cloned.1.call-update) | async-done | bytes 839824 | tf_op jit(solution)/shard_map/reduce_scatter | solution.py:159
  546.3 11.9 all-reduce.2
  776.1 14.4 %reduce-scatter.33.cloned.1.call-done = bf16[729,288]{0,1:T(8,128)(2,1)} async-done(((bf16[729,1152]{0,1:T(8,128)(2,1)}), bf16[729,288]{0,1:T(8,128)(2,1)}) %reduce-scatter.33.cloned.1.call-update) | async-done | bytes 419920 | tf_op jit(solution)/shard_map/reduce_scatter | solution.py:210
  790.5 32.0 %reduce-scatter.41.cloned.1.call-done = bf16[729,288]{0,1:T(8,128)(2,1)} async-done(((bf16[729,1152]{0,1:T(8,128)(2,1)}), bf16[729,288]{0,1:T(8,128)(2,1)}) %reduce-scatter.41.cloned.1.call-update) | async-done | bytes 419920 | tf_op jit(solution)/shard_map/reduce_scatter | solution.py:210
  827.5 40.5 %all-reduce = (f32[288]{0:T(512)}, f32[288]{0:T(512)}, f32[288]{0:T(512)}, f32[288]{0:T(512)}, f32[288]{0:T(512)}, /*index=5*/f32[288]{0:T(512)}, f32[288]{0:T(512)}, f32[1076]{0:T(1024)}, f32[288]{0:T(512)}) all-reduce(f32[288]{0:T(512)} %add_add_fusion.8, f32[288]{0:T(512)} %add_add_fusion.7, ...), channel_id=1, replica_groups=mesh['dp'=8,'tensor'=4] {'dp'}, use_global_device_ids=true, to_apply=%region_60.62 | all-reduce | flops 3380 | bytes 27040 | tf_op jit(solution)/shard_map/psum | solution.py:249
  868.0 12.2 all-reduce.1
  889.1 42.0 %reduce-scatter.53.cloned.1.call-done = f32[1076,144]{0,1:T(8,128)} async-done(((f32[1076,1152]{0,1:T(8,128)}), f32[1076,144]{0,1:T(8,128)}) %reduce-scatter.53.cloned.1.call-update) | async-done | bytes 619792 | tf_op jit(solution)/shard_map/reduce_scatter | solution.py:247
  931.1 108.3 %reduce-scatter.51.cloned.1.call-done = f32[144,1076]{1,0:T(8,128)} async-done(((f32[1152,1076]{1,0:T(8,128)}), f32[144,1076]{1,0:T(8,128)}) %reduce-scatter.51.cloned.1.call-update) | async-done | bytes 619792 | tf_op jit(solution)/shard_map/reduce_scatter | solution.py:243
  1039.4 70.0 %reduce-scatter.49.cloned.1.call-done = f32[288,144]{0,1:T(8,128)} async-done(((f32[288,1152]{0,1:T(8,128)}), f32[288,144]{0,1:T(8,128)}) %reduce-scatter.49.cloned.1.call-update) | async-done | bytes 165904 | tf_op jit(solution)/shard_map/reduce_scatter | solution.py:246
  1109.5 69.7 %reduce-scatter.47.cloned.1.call-done = f32[144,288]{1,0:T(8,128)} async-done(((f32[1152,288]{1,0:T(8,128)}), f32[144,288]{1,0:T(8,128)}) %reduce-scatter.47.cloned.1.call-update) | async-done | bytes 165904 | tf_op jit(solution)/shard_map/reduce_scatter | solution.py:242
  1179.2 69.1 %reduce-scatter.45.cloned.1.call-done = f32[144,288]{1,0:T(8,128)} async-done(((f32[1152,288]{1,0:T(8,128)}), f32[144,288]{1,0:T(8,128)}) %reduce-scatter.45.cloned.1.call-update) | async-done | bytes 165904 | tf_op jit(solution)/shard_map/reduce_scatter | solution.py:241
  1248.3 70.0 %reduce-scatter.43.cloned.1.call-done = f32[144,288]{1,0:T(8,128)} async-done(((f32[1152,288]{1,0:T(8,128)}), f32[144,288]{1,0:T(8,128)}) %reduce-scatter.43.cloned.1.call-update) | async-done | bytes 165904 | tf_op jit(solution)/shard_map/reduce_scatter | solution.py:240
  (498 shorter events, 417.8 us)
Async XLA Ops:
  8.1 135.6 %all-gather.32.cloned.1.call-start = ((), (), s32[]{:S(2)}) async-start(), calls=%async_computation.43 | async-start | bytes 2211840 | tf_op jit(solution)/shard_map/all_gather | solution.py:91
  10.6 152.5 %all-gather.30.cloned.1.call-start = ((), (), s32[]{:S(2)}) async-start(), calls=%async_computation.42 | async-start | bytes 2211840 | tf_op jit(solution)/shard_map/all_gather | solution.py:91
  11.3 172.1 %all-gather.28.cloned.1.call-start = ((), (), s32[]{:S(2)}) async-start(), calls=%async_computation.41 | async-start | bytes 2211840 | tf_op jit(solution)/shard_map/all_gather | solution.py:91
  12.1 195.7 %reduce-scatter.27.cloned.1.call-start = ((), (), s32[]{:S(2)}) async-start(), calls=%async_computation.24 | async-start | bytes 4423680 | tf_op jit(solution)/shard_map/reduce_scatter | solution.py:127
  183.0 108.0 %reduce-scatter.19.cloned.1.call-start = ((), (), s32[]{:S(2)}) async-start(), calls=%async_computation.18 | async-start | bytes 4423680 | tf_op jit(solution)/shard_map/reduce_scatter | solution.py:127
  203.3 142.3 %all-gather.18.cloned.1.call-start = ((), (), s32[]{:S(2)}) async-start(), calls=%async_computation.19 | async-start | bytes 2985984 | tf_op jit(solution)/shard_map/all_gather | solution.py:20
  203.8 148.9 %all-gather.38.cloned.1.call-start = ((), (), s32[]{:S(2)}) async-start(), calls=%async_computation.46 | async-start | bytes 2211840 | tf_op jit(solution)/shard_map/all_gather | solution.py:92
  206.3 151.7 %all-gather.20.cloned.1.call-start = ((), (), s32[]{:S(2)}) async-start(), calls=%async_computation.20 | async-start | bytes 2985984 | tf_op jit(solution)/shard_map/all_gather | solution.py:24
  206.9 217.9 %all-gather.36.cloned.1.call-start = ((), (), s32[]{:S(2)}) async-start(), calls=%async_computation.45 | async-start | bytes 2211840 | tf_op jit(solution)/shard_map/all_gather | solution.py:92
  207.7 279.9 %all-gather.34.cloned.1.call-start = ((), (), s32[]{:S(2)}) async-start(), calls=%async_computation.44 | async-start | bytes 2211840 | tf_op jit(solution)/shard_map/all_gather | solution.py:92
  322.0 181.1 %reduce-scatter.39.cloned.1.call-start = ((), (), s32[]{:S(2)}) async-start(), calls=%async_computation.32 | async-start | bytes 4423680 | tf_op jit(solution)/shard_map/reduce_scatter | solution.py:159
  372.1 131.0 %reduce-scatter.35.cloned.1.call-start = ((), (), s32[]{:S(2)}) async-start(), calls=%async_computation.29 | async-start | bytes 4423680 | tf_op jit(solution)/shard_map/reduce_scatter | solution.py:159
  572.9 187.6 %reduce-scatter.29.cloned.1.call-start = ((), (), s32[]{:S(2)}) async-start(), calls=%async_computation.25 | async-start | bytes 2211840 | tf_op jit(solution)/shard_map/reduce_scatter | solution.py:145
  579.7 180.9 %reduce-scatter.25.cloned.1.call-start = ((), (), s32[]{:S(2)}) async-start(), calls=%async_computation.23 | async-start | bytes 2211840 | tf_op jit(solution)/shard_map/reduce_scatter | solution.py:145
  586.4 174.2 %reduce-scatter.21.cloned.1.call-start = ((), (), s32[]{:S(2)}) async-start(), calls=%async_computation.21 | async-start | bytes 2211840 | tf_op jit(solution)/shard_map/reduce_scatter | solution.py:145
  596.5 179.6 %reduce-scatter.37.cloned.1.call-start = ((), (), s32[]{:S(2)}) async-start(), calls=%async_computation.31 | async-start | bytes 2211840 | tf_op jit(solution)/shard_map/reduce_scatter | solution.py:210
  659.9 130.7 %reduce-scatter.33.cloned.1.call-start = ((), (), s32[]{:S(2)}) async-start(), calls=%async_computation.28 | async-start | bytes 2211840 | tf_op jit(solution)/shard_map/reduce_scatter | solution.py:210
  682.8 139.7 %reduce-scatter.41.cloned.1.call-start = ((), (), s32[]{:S(2)}) async-start(), calls=%async_computation.34 | async-start | bytes 2211840 | tf_op jit(solution)/shard_map/reduce_scatter | solution.py:210
  707.2 223.9 %reduce-scatter.53.cloned.1.call-start = ((), (), s32[]{:S(2)}) async-start(), calls=%async_computation.40 | async-start | bytes 5971968 | tf_op jit(solution)/shard_map/reduce_scatter | solution.py:247
  720.2 319.2 %reduce-scatter.51.cloned.1.call-start = ((), (), s32[]{:S(2)}) async-start(), calls=%async_computation.39 | async-start | bytes 5971968 | tf_op jit(solution)/shard_map/reduce_scatter | solution.py:243
  734.6 374.9 %reduce-scatter.49.cloned.1.call-start = ((), (), s32[]{:S(2)}) async-start(), calls=%async_computation.38 | async-start | bytes 1990656 | tf_op jit(solution)/shard_map/reduce_scatter | solution.py:246
  742.4 436.8 %reduce-scatter.47.cloned.1.call-start = ((), (), s32[]{:S(2)}) async-start(), calls=%async_computation.37 | async-start | bytes 1990656 | tf_op jit(solution)/shard_map/reduce_scatter | solution.py:242
  749.7 498.6 %reduce-scatter.45.cloned.1.call-start = ((), (), s32[]{:S(2)}) async-start(), calls=%async_computation.36 | async-start | bytes 1990656 | tf_op jit(solution)/shard_map/reduce_scatter | solution.py:241
  759.2 559.2 %reduce-scatter.43.cloned.1.call-start = ((), (), s32[]{:S(2)}) async-start(), calls=%async_computation.35 | async-start | bytes 1990656 | tf_op jit(solution)/shard_map/reduce_scatter | solution.py:240
  (144 other events, 1962.0 us)
Sparse Core Ops, SparseCore 0:
  11.0 23.4 all-gather.31
  36.6 20.7 all-gather.29
  59.6 20.7 all-gather.27
  162.9 41.7 reduce-scatter.26
  207.3 40.4 reduce-scatter.22
  250.3 40.6 reduce-scatter.18
  563.4 21.4 all-gather.23
  587.0 20.7 all-gather.21
  609.9 20.7 all-gather.25
  633.1 29.3 reduce-scatter.28
  665.3 29.3 reduce-scatter.24
  697.1 29.3 reduce-scatter.20
  729.3 29.3 reduce-scatter.36
  761.1 29.3 reduce-scatter.32
  793.1 29.3 reduce-scatter.40
  826.6 104.5 reduce-scatter.52
  935.6 103.8 reduce-scatter.50
  1043.3 66.1 reduce-scatter.48
  1113.9 65.2 reduce-scatter.46
  1183.0 65.2 reduce-scatter.44
  1252.7 65.5 reduce-scatter.42
Sparse Core Ops, SparseCore 1:
  206.1 56.4 all-gather.17
  264.6 36.0 all-gather.37
  303.0 55.0 all-gather.19
  359.7 20.3 all-gather.35
  382.4 26.6 all-gather.33
  411.7 44.8 reduce-scatter.38
  459.0 40.3 reduce-scatter.34
  502.0 40.2 reduce-scatter.30
